TPU v7x, 32 devices: a whole 2x2x4 slice. The times are simulated.
32 devices in a mesh: lat: 4 (over z), lon: 8 (over y, x, core).
Axes of the slice: x: 2, y: 2, z: 4, core: 2. Of those that a mesh axis runs over, the one named last changes fastest.
Arguments:
- tokens: bfloat16 [8, 12, 128, 384], P(None, 'lat', 'lon'), may hold values from -6 to 6
- gain_attn: float32 [384], replicated, may hold values from 0.25 to 1.75
- w_qkv: bfloat16 [384, 1152], replicated, may hold values from -0.3125 to 0.3125
- esb: float32 [12, 12, 5], P('lat'), may hold values from -4 to 250
- w_out: bfloat16 [384, 384], replicated, may hold values from -0.3125 to 0.3125
- gain_mlp: float32 [384], replicated, may hold values from 0.25 to 1.75
- w_up: bfloat16 [384, 1536], replicated, may hold values from -0.3125 to 0.3125
- w_down: bfloat16 [1536, 384], replicated, may hold values from -0.15625 to 0.15625
- widths: int32 [4], replicated, may hold values from 1 to 8, as said below
- shifts: int32 [4], replicated, may hold values from 0 to 7
Outputs:
- result: bfloat16 [8, 12, 128, 384], P(None, 'lat', 'lon')
Inputs may be any that keep to these rules, and one draw needn't show every extreme that they name: `widths`: each width is a power of two; some band has 8 (the whole circle) and some band has 1.
All inputs are finite; a program needn't handle non-finite values.
Results may differ from a plain program's by a relative error of at most 0.011.
Values may be sent and summed in bfloat16 or wider, within the bound.
A program may use at most 704 MiB of HBM per device.

v0:
```python
import jax
import jax.numpy as jnp
from jax import lax
from jax.sharding import PartitionSpec as P

EPS = 1e-05
NEG = -1e30


def with_halo(cells, sides, width):
    for axis, dim in sides:
        count = lax.axis_size(axis)
        ends = count - 1
        head = lax.slice_in_dim(cells, 0, width, axis=dim)
        tail = lax.slice_in_dim(cells, cells.shape[dim] - width, cells.shape[dim], axis=dim)
        cells = jnp.concatenate(
            [
                lax.ppermute(tail, axis, [(i, (i + 1) % count) for i in range(ends)]),
                cells,
                lax.ppermute(head, axis, [((i + 1) % count, i) for i in range(ends)]),
            ],
            axis=dim,
        )
    return cells


def normalize(rows, gain):
    mean = jnp.mean(rows, axis=-1, keepdims=True)
    centred = rows - mean
    spread = jnp.mean(centred * centred, axis=-1, keepdims=True)
    return centred * lax.rsqrt(spread + EPS) * gain


def attend_block(carry, queries, bias_q, block, rows_ok, col_ok, scale):
    count, heads, dim = queries.shape
    levels, ext, ncols, twice = block.shape
    width = twice // 2
    keys = block[..., :width].reshape(-1, heads, dim)
    values = block[..., width:].reshape(-1, heads, dim)
    valid = rows_ok[:, None] & col_ok[None, :]
    valid_flat = jnp.broadcast_to(valid[None], (levels, ext, ncols)).reshape(-1)
    top, total, acc = carry
    scores = jnp.einsum("qhd,khd->hqk", queries, keys, preferred_element_type=jnp.float32) * scale
    scores = scores.reshape(heads, count, levels, ext, ncols) + bias_q[:, :, None, :, None]
    scores = jnp.where(valid_flat[None, None, :], scores.reshape(heads, count, -1), NEG)
    new_top = jnp.maximum(top, jnp.max(scores, axis=2))
    weights = jnp.where(valid_flat[None, None, :], jnp.exp(scores - new_top[:, :, None]), 0.0)
    total = jnp.sum(weights, axis=2)
    update = jnp.einsum(
        "hqk,khd->hqd", weights.astype(jnp.bfloat16), values, preferred_element_type=jnp.float32
    )
    acc = update
    return (new_top, total, acc)


def shards(tokens, gain_attn, w_qkv, esb, w_out, gain_mlp, w_up, w_down, widths, shifts):
    levels, rows, cols, width = tokens.shape
    heads = esb.shape[1]
    ext = esb.shape[2]
    rim = (ext - rows) // 2
    dim = width // heads
    n_lon = lax.axis_size("lon")
    n_lat = lax.axis_size("lat")
    band = lax.axis_index("lat")
    place = lax.axis_index("lon")
    wide = widths[band]
    offset = shifts[band]
    home = (place - offset) % n_lon // wide
    flat = tokens.reshape(-1, width)
    count = flat.shape[0]
    h_one = normalize(flat.astype(jnp.float32), gain_attn).astype(jnp.bfloat16)
    w_query = w_qkv[:, :width]
    w_pair = w_qkv[:, width:]
    lat_rows = band * rows - rim + jnp.arange(ext, dtype=jnp.int32)
    rows_ok = (lat_rows >= 0) & (lat_rows < rows * n_lat)
    bias_rows = esb.transpose(1, 0, 2)
    bias_q = jnp.broadcast_to(
        bias_rows[:, None, :, None, :], (heads, levels, rows, cols, ext)
    ).reshape(heads, count, ext)
    scale = dim ** (-0.5)
    start_state = (
        jnp.full((heads, count), NEG, jnp.float32),
        jnp.zeros((heads, count), jnp.float32),
        jnp.zeros((heads, count, dim), jnp.float32),
    )
    query_rows = jnp.dot(h_one, w_query, preferred_element_type=jnp.float32).astype(jnp.bfloat16)
    queries = query_rows.reshape(count, heads, dim)
    normed = h_one.reshape(levels, rows, cols, width)
    shape = normed.shape
    pairs = jnp.dot(normed.reshape(-1, width), w_pair, preferred_element_type=jnp.float32).astype(
        jnp.bfloat16
    )
    paired = pairs.reshape(shape[0], shape[1], shape[2], 2 * width)
    framed = with_halo(paired, (("lat", 1),), rim)
    block = lax.all_gather(framed, "lon", axis=2, tiled=True)
    ncols = block.shape[2]
    source = jnp.arange(ncols, dtype=jnp.int32) // cols
    col_ok = (source - offset) % n_lon // wide == home

    def take(state):
        return attend_block(state, queries, bias_q, block, rows_ok, col_ok, scale)

    def leave(state):
        return state

    top, total, acc = lax.cond(jnp.any(col_ok), take, leave, start_state)
    attn = (acc / total[:, :, None]).transpose(1, 0, 2).reshape(count, width).astype(jnp.bfloat16)
    mixed = (
        flat.astype(jnp.float32) + jnp.dot(attn, w_out, preferred_element_type=jnp.float32)
    ).astype(jnp.bfloat16)
    h_two = normalize(mixed.astype(jnp.float32), gain_mlp).astype(jnp.bfloat16)
    hidden = jax.nn.gelu(
        jnp.dot(h_two, w_up, preferred_element_type=jnp.float32), approximate=False
    ).astype(jnp.bfloat16)
    result = mixed.astype(jnp.float32) + jnp.dot(hidden, w_down, preferred_element_type=jnp.float32)
    return result.astype(jnp.bfloat16).reshape(tokens.shape)


def solution(mesh):
    placed = (
        P(None, "lat", "lon", None),
        P(),
        P(),
        P("lat", None, None),
        P(),
        P(),
        P(),
        P(),
        P(),
        P(),
    )
    return jax.shard_map(
        shards, mesh=mesh, in_specs=placed, out_specs=P(None, "lat", "lon", None), check_vma=False
    )
```

profile of v0, /device:TPU:1, one launch (start us, length us, event | category | flops | bytes accessed | tf_op | source)
XLA Modules:
  0.0 400.0 jit_solution(13113878851310743604)
XLA Ops:
  6.5 1.2 convert_reduce_fusion
  7.7 1.2 multiply_reduce_fusion.1
  9.2 1.1 fusion.22
  10.3 1.5 convolution_convert_fusion
  11.9 1.3 collective-permute-start.1
  13.2 4.8 %collective-permute-start = (bf16[8,1,16,768]{3,2,1,0:T(8,128)(2,1)S(1)}, bf16[8,1,16,768]{3,2,1,0:T(8,128)(2,1)S(1)}, u32[]{:S(2)}, u32[]{:S(2)}) collective-permute-start(bf16[8,1,16,768]{3,2,1,0:T(8,128)(2,1)S(1)} %get-tuple-element.103), channel_id=1, source_target_pairs={{0,8},{8,16},{16,24},{1,9},{9,17},{17,25},{2,10},{10,18},{18,26},{... | collective-permute-start | bytes 589832 | tf_op jit(solution)/shard_map/ppermute | solution.py:18
  18.0 2.5 collective-permute-done.1
  20.5 1.0 collective-permute-done
  21.7 1.2 copy.31
  26.5 2.0 fusion.65
  29.3 1.3 convolution_convert_fusion.1
  30.6 48.3 %all-gather.2.cloned.1.call-done = bf16[8,5,128,768]{3,0,1,2:T(8,128)(2,1)} async-done(((bf16[8,5,16,768]{3,0,1,2:T(8,128)(2,1)}), bf16[8,5,128,768]{3,0,1,2:T(8,128)(2,1)}) %all-gather.2.cloned.1.call-update) | async-done | bytes 7864336 | tf_op jit(solution)/shard_map/all_gather | solution.py:95
  78.9 304.5 %conditional.1 = (f32[12,384]{1,0:T(8,128)}, f32[12,384,32]{1,2,0:T(8,128)}) conditional(s32[]{:T(128)} %convert_element_type.55, () %tuple.19, (s32[]{:T(128)}, s32[5]{0:T(128)S(1)}, pred[128]{0:T(512)(128)(4,1)S(1)}, bf16[384,384]{1,0:T(8,128)(2,1)S(1)}, bf16[8,5,128,768]{3,0,1,2:T(8,128)(2,1)}, /*index=5*/f32[12,3,5]{1,0,2:T(8,128)S(1)}) %tuple.34), branch_computations={%region_3.4_spmd, %region_4.7_spmd} | conditional | flops 3255824384 | bytes 717824128 | solution.py:106
  79.8 29.5 %add.60 = f32[12,384,8,5,128]{1,4,3,2,0:T(8,128)} broadcast(f32[12,384,5]{1,2,0:T(8,128)S(1)} %copy.29), dimensions={0,1,3} | broadcast | bytes 94464000 | tf_op jit(solution)/shard_map/cond/branch_1_fun/add | solution.py:44
  109.3 91.1 %copy.30 = f32[12,384,5120]{2,1,0:T(8,128)} copy(f32[12,384,5120]{1,2,0:T(8,128)} %bitcast.1) | data formatting | bytes 188743680 | tf_op jit(solution)/shard_map/cond/branch_1_fun/add | solution.py:44
  200.6 23.0 %copy.34 = bf16[8,5,128,768]{2,1,0,3:T(8,128)(2,1)} copy(bf16[8,5,128,768]{3,0,1,2:T(8,128)(2,1)} %get-tuple-element.95) | data formatting | bytes 15728640 | tf_op jit(solution)/shard_map
  223.7 11.4 %fusion.67 = (bf16[8,5,128,384]{2,1,0,3:T(8,128)(2,1)}, bf16[8,5,128,384]{2,1,0,3:T(8,128)(2,1)}) fusion(bf16[8,5,128,768]{2,1,0,3:T(8,128)(2,1)} %copy.34), kind=kLoop, calls=%fused_computation.98 | loop fusion | bytes 15728640 | tf_op jit(solution)/shard_map/cond/branch_1_fun/slice | solution.py:39
  235.0 9.6 %reshape.111 = bf16[5120,12,32]{0,2,1:T(8,128)(2,1)} reshape(bf16[8,5,128,384]{2,1,0,3:T(8,128)(2,1)} %get-tuple-element.100) | data formatting | bytes 7864320 | tf_op jit(solution)/shard_map/cond/branch_1_fun/reshape | solution.py:38
  244.8 65.5 %fusion.68 = (f32[12,384]{1,0:T(8,128)S(1)}, f32[12,384,5120]{2,1,0:T(8,128)}) fusion(f32[12,384,5120]{2,1,0:T(8,128)} %copy.30, bf16[384,12,32]{0,2,1:T(8,128)(2,1)S(1)} %bitcast.38, bf16[5120,12,32]{0,2,1:T(8,128)(2,1)} %reshape.111, pred[5120]{0:T(1024)(128)(4,1)S(1)} %broadcast_in_dim.59), kind=kOutput, calls=%fused_computation.99 | convolution fusion | flops 1604316672 | bytes 192994304 | tf_op jit(solution)/shard_map/cond/branch_1_fun/qhd,khd->hqk/dot_general | solution.py:43
  310.3 30.0 %fusion.1 = f32[12,384]{1,0:T(8,128)} fusion(f32[12,384,5120]{2,1,0:T(8,128)} %get-tuple-element.102, f32[12,384]{1,0:T(8,128)S(1)} %broadcast_maximum_fusion, pred[5120]{0:T(1024)(128)(4,1)S(1)} %broadcast_in_dim.59), kind=kLoop, calls=%fused_computation.3 | loop fusion | flops 70774272 | bytes 94413824 | tf_op jit(solution)/shard_map/cond/branch_1_fun/reduce_sum | solution.py:48
  340.3 9.6 %reshape.112 = bf16[5120,12,32]{0,2,1:T(8,128)(2,1)} reshape(bf16[8,5,128,384]{2,1,0,3:T(8,128)(2,1)} %get-tuple-element.99) | data formatting | bytes 7864320 | tf_op jit(solution)/shard_map/cond/branch_1_fun/reshape | solution.py:39
  349.9 33.5 %fusion.2 = f32[12,384,32]{1,2,0:T(8,128)} fusion(bf16[5120,12,32]{0,2,1:T(8,128)(2,1)} %reshape.112, f32[12,384,5120]{2,1,0:T(8,128)} %get-tuple-element.102, f32[12,384]{1,0:T(8,128)S(1)} %broadcast_maximum_fusion, pred[5120]{0:T(1024)(128)(4,1)S(1)} %broadcast_in_dim.59), kind=kOutput, calls=%fused_computation.4 | convolution fusion | flops 1580728320 | bytes 98917376 | tf_op jit(solution)/shard_map/cond/branch_1_fun/hqk,khd->hqd/dot_general | solution.py:49
  383.4 1.1 divide_convert_fusion
  385.3 7.9 %fusion.18 = bf16[384,384]{1,0:T(8,128)(2,1)} fusion(f32[384,384]{1,0:T(8,128)S(1)} %get-tuple-element.106, bf16[1536,384]{1,0:T(8,128)(2,1)S(1)} %copy-done, bf16[384,1536]{1,0:T(8,128)(2,1)} %param.18, f32[384]{0:T(512)S(1)} %copy-done.4, f32[384]{0:T(512)S(1)} %add_rsqrt_fusion.1, f32[384]{0:T(512)S(1)} %broadcast_multiply_fusion.1), kind=kOutput, calls=%fused_computation.35 | convolution fusion | flops 945192960 | bytes 3248640 | tf_op jit(solution)/shard_map/dot_general | solution.py:115
  (39 shorter events, 3.6 us)
Async XLA Ops:
  6.5 378.7 %copy-start = (bf16[1536,384]{1,0:T(8,128)(2,1)S(1)}, bf16[1536,384]{1,0:T(8,128)(2,1)}, u32[]{:S(2)}) copy-start(bf16[1536,384]{1,0:T(8,128)(2,1)} %param.19) | copy-start | bytes 3538948
  6.5 72.3 %all-gather.2.cloned.1.call-start = ((), (), s32[]{:S(2)}) async-start(), calls=%async_computation | async-start | bytes 8847360 | tf_op jit(solution)/shard_map/all_gather | solution.py:95
  11.9 8.7 %collective-permute-start.1 = (bf16[8,1,16,768]{3,2,1,0:T(8,128)(2,1)S(1)}, bf16[8,1,16,768]{3,2,1,0:T(8,128)(2,1)S(1)}, u32[]{:S(2)}, u32[]{:S(2)}) collective-permute-start(bf16[8,1,16,768]{3,2,1,0:T(8,128)(2,1)S(1)} %get-tuple-element.104), channel_id=1, source_target_pairs={{8,0},{16,8},{24,16},{9,1},{17,9},{25,17},{10,2},{18,10},{26,18},{... | collective-permute-start | bytes 589832 | tf_op jit(solution)/shard_map/ppermute | solution.py:20
  13.2 9.8 %copy-start.5 = (s32[4]{0:T(128)S(1)}, s32[4]{0:T(128)}, u32[]{:S(2)}) copy-start(s32[4]{0:T(128)} %param.21) | copy-start | bytes 52
  13.2 11.0 %copy-start.6 = (s32[4]{0:T(128)S(1)}, s32[4]{0:T(128)}, u32[]{:S(2)}) copy-start(s32[4]{0:T(128)} %param.20) | copy-start | bytes 52
  13.2 16.0 %copy-start.3 = (f32[3,12,5]{1,0,2:T(4,128)S(1)}, f32[3,12,5]{1,0,2:T(4,128)}, u32[]{:S(2)}) copy-start(f32[3,12,5]{1,0,2:T(4,128)} %param.15) | copy-start | bytes 2164
  13.2 8.4 %collective-permute-start = (bf16[8,1,16,768]{3,2,1,0:T(8,128)(2,1)S(1)}, bf16[8,1,16,768]{3,2,1,0:T(8,128)(2,1)S(1)}, u32[]{:S(2)}, u32[]{:S(2)}) collective-permute-start(bf16[8,1,16,768]{3,2,1,0:T(8,128)(2,1)S(1)} %get-tuple-element.103), channel_id=1, source_target_pairs={{0,8},{8,16},{16,24},{1,9},{9,17},{17,25},{2,10},{10,18},{18,26},{... | collective-permute-start | bytes 589832 | tf_op jit(solution)/shard_map/ppermute | solution.py:18
  78.9 305.6 %copy-start.1 = (bf16[8,3,16,384]{3,2,1,0:T(8,128)(2,1)S(1)}, bf16[8,3,16,384]{3,2,1,0:T(8,128)(2,1)}, u32[]{:S(2)}) copy-start(bf16[8,3,16,384]{3,2,1,0:T(8,128)(2,1)} %param.12) | copy-start | bytes 884740
  78.9 305.6 %copy-start.2 = (bf16[384,384]{1,0:T(8,128)(2,1)S(1)}, bf16[384,384]{1,0:T(8,128)(2,1)}, u32[]{:S(2)}) copy-start(bf16[384,384]{1,0:T(8,128)(2,1)} %param.16) | copy-start | bytes 884740
  383.4 1.9 copy-start.4
Sparse Core Ops, SparseCore 0:
  23.1 55.7 all-gather.1
where the time goes:
time: 402 us; the launch traced here: 400 us
  local copies, waits for them, and re-layouts  178 us (44%)
  matrix products  110 us (27%)
  waiting for transfers between devices  51.8 us (13%)
  other arithmetic  37.1 us (9%)
  between operations  16.6 us (4%)
  starting transfers between devices  6.1 us (2%)
    add x4, local copies, waits for them, and re-layouts, attend_block(): scores.reshape(heads, count, levels, ext, ncols)  121 us
    dot_general x1, matrix products, attend_block(): jnp.einsum('qhd,khd->hqk', queries, keys, preferred_element_type=jnp.floa...  65.5 us
    all_gather x1, waiting for transfers between devices, shards(): block = lax.all_gather(framed, 'lon', axis=2, tiled=True)  48.3 us
    dot_general x1, matrix products, attend_block(): jnp.einsum('hqk,khd->hqd', weights.astype(jnp.bfloat16), values, preferre...  33.5 us
    reduce_sum x1, other arithmetic, attend_block(): total = jnp.sum(weights, axis=2)  30 us
    another operation x2, local copies, waits for them, and re-layouts  23.3 us
    slice x1, local copies, waits for them, and re-layouts, attend_block(): values = block[..., width:].reshape(-1, heads, dim)  11.4 us
    reshape x1, local copies, waits for them, and re-layouts, attend_block(): keys = block[..., :width].reshape(-1, heads, dim)  9.64 us
  transfers between devices with their start and end apart: 3, of which 3 were waited for; matrix products, arithmetic and copies ran while one was open for 1% of the time, Pallas kernels for 0%

commit v1 on v0

v1 whole, which is shorter than its diff:
```python
import functools
import math

import jax
import jax.numpy as jnp
from jax import lax
from jax.experimental import pallas as pl
from jax.experimental.pallas import tpu as pltpu
from jax.sharding import PartitionSpec as P

EPS = 1e-05
NEG = -1e30
LOW = -3e38
LANES = 128
F32 = jnp.float32
BF16 = jnp.bfloat16
MESH = pl.DeviceIdType.MESH


def normalize(rows, gain):
    mean = jnp.mean(rows, axis=-1, keepdims=True)
    centred = rows - mean
    spread = jnp.mean(centred * centred, axis=-1, keepdims=True)
    return centred * lax.rsqrt(spread + EPS) * gain


def dot(a, b):
    return jnp.dot(a, b, preferred_element_type=F32)


def flip(index, bit):
    return index + bit - 2 * bit * ((index // bit) % 2)


def start_queries(h_one, esb_ref, w_qkv_ref, q_aug, heads, dim, rows):
    count, width = h_one.shape
    per_row = count // rows
    queries = dot(h_one, w_qkv_ref[:, :width]).astype(BF16).astype(F32)
    queries = queries * (dim ** (-0.5) * math.log2(math.e))
    lane = lax.broadcasted_iota(jnp.int32, (per_row, LANES), 1)
    group = LANES // dim
    biases = [bias_lanes(esb_ref[r], dim) for r in range(rows)]
    for h in range(heads):
        at = h // group * LANES
        turn = h % group * dim
        for r in range(rows):
            piece = queries[r * per_row : (r + 1) * per_row, at : at + LANES]
            high = piece.astype(BF16).astype(F32)
            low = piece - high
            if turn:
                high = pltpu.roll(high, LANES - turn, 1)
            if turn != dim:
                low = pltpu.roll(low, (dim - turn) % LANES, 1)
            bias = jnp.broadcast_to(biases[r][h : h + 1, :], (per_row, LANES))
            packed = jnp.where(lane < dim, high, jnp.where(lane < 2 * dim, low, bias))
            q_aug[h, r * per_row : (r + 1) * per_row, :] = packed.astype(BF16)


def start_state(k_aug, v_aug, top, acc, heads, dim, ext, rows):
    span = k_aug.shape[2]
    per_row = LANES
    row = lax.broadcasted_iota(jnp.int32, (16, span), 0)
    key = lax.broadcasted_iota(jnp.int32, (16, span), 1)
    place = (key // per_row + (ext - rows) // 2) % ext
    hot = ((row % ext) == place) & (row < 3 * ext)
    k_aug[:, 2 * dim + 16 :, :] = jnp.zeros((heads, k_aug.shape[1] - 2 * dim - 16, span), BF16)
    v_aug[:, :, LANES:] = jnp.ones((v_aug.shape[0], span, LANES), BF16)
    top[...] = jnp.full(top.shape, LOW, F32)
    acc[...] = jnp.zeros(acc.shape, F32)
    return hot.astype(F32), row


def attend(block, mask, hot, row, w_kt, w_qkv_ref, q_aug, k_aug, v_aug, scores, probs, top, acc, heads, dim):
    span, width = block.shape
    count = q_aug.shape[1]
    group = LANES // dim
    extra = jnp.where(row == 15, jnp.broadcast_to(mask, row.shape), hot).astype(BF16)
    for g in range(width // LANES):
        keys = lax.dot_general(
            w_kt[g * LANES : (g + 1) * LANES, :], block, (((1,), (1,)), ((), ())), preferred_element_type=F32
        ).astype(BF16)
        for j in range(group):
            h = g * group + j
            head = keys[j * dim : (j + 1) * dim, :]
            k_aug[h, :dim, :] = head
            k_aug[h, dim : 2 * dim, :] = head
            k_aug[h, 2 * dim : 2 * dim + 16, :] = extra
    values = dot(block, w_qkv_ref[:, 2 * width :]).astype(BF16)
    for g in range(width // LANES):
        v_aug[g, :, :LANES] = values[:, g * LANES : (g + 1) * LANES]

    def product(h, slot):
        scores[slot][...] = dot(q_aug[h], k_aug[h])

    def soften(h, slot):
        step = 32
        for at in range(0, count, step):
            s = scores[slot][at : at + step, :]
            old = top[h, at : at + step, :]
            new = jnp.maximum(old, jnp.max(s, axis=1, keepdims=True))
            top[h, at : at + step, :] = new
            alpha = jnp.exp2(old - new)
            wide = jnp.concatenate([new] * (span // LANES), axis=1)
            probs[slot][at : at + step, :] = jnp.exp2(s - wide).astype(BF16)
            acc[h, at : at + step, :] = acc[h, at : at + step, :] * jnp.concatenate([alpha, alpha], axis=1)
        acc[h] += dot(probs[slot][...], v_aug[h // group])

    product(0, 0)

    def pair(i, carry):
        product(2 * i + 1, 1)
        soften(2 * i, 0)
        product(jnp.minimum(2 * i + 2, heads - 1), 0)
        soften(2 * i + 1, 1)
        return carry

    lax.fori_loop(0, heads // 2, pair, 0)


def finish(flat, acc, w_out_ref, gain_mlp_ref, w_up_ref, w_down_ref, heads, dim):
    count, width = flat.shape
    group = LANES // dim
    lane = lax.broadcasted_iota(jnp.int32, (count, LANES), 1)
    parts = []
    for g in range(width // LANES):
        part = jnp.zeros((count, LANES), F32)
        for j in range(group):
            h = g * group + j
            part = jnp.where(lane // dim == j, acc[h, :, :LANES] / acc[h, :, LANES:], part)
        parts.append(part.astype(BF16))
    attn = jnp.concatenate(parts, axis=1)
    mixed = (flat.astype(F32) + dot(attn, w_out_ref[...])).astype(BF16)
    h_two = normalize(mixed.astype(F32), gain_mlp_ref[...]).astype(BF16)
    up = dot(h_two, w_up_ref[...])
    hidden = (0.5 * up * (1.0 + lax.erf(up * math.sqrt(0.5)))).astype(BF16)
    return (mixed.astype(F32) + dot(hidden, w_down_ref[...])).astype(BF16)


def by_row(tokens_ref, rows, width):
    return jnp.concatenate([tokens_ref[:, r].reshape(-1, width) for r in range(rows)], axis=0)


def layer_kernel(heads, dim, ext, n_lon, n_lat, remote, *refs):
    tokens_ref, esb_ref, gain_attn_ref, gain_mlp_ref, widths_ref, shifts_ref = refs[:6]
    weights, refs = refs[6:10], refs[10:]
    if remote:
        out_ref, blocks, send, recv = refs[:4]
        refs = refs[4:]
    else:
        blocks, out_ref = refs[:2]
        refs = refs[2:]
    q_aug, k_aug, v_aug, scores_a, scores_b, probs_a, probs_b, top, acc, w_kt = refs[:10]
    w_qkv_ref, w_out_ref, w_up_ref, w_down_ref, loads = refs[10:]
    levels, rows, cols, width = tokens_ref.shape
    per_row = levels * cols
    rim = (ext - rows) // 2
    span = k_aug.shape[2]
    band = lax.axis_index("lat")
    place = lax.axis_index("lon")
    core = place % 2
    other = 1 - core
    fetch = [
        pltpu.make_async_copy(weights[i], (w_qkv_ref, w_out_ref, w_up_ref, w_down_ref)[i], loads.at[i])
        for i in range(4)
    ]
    for copy in fetch:
        copy.start()

    sibling, over_x, over_y = flip(place, 1), flip(place, 2), flip(place, 4)
    has_above, has_below = band < n_lat - 1, band > 0

    if remote:
        barrier = pltpu.get_barrier_semaphore()
        for target in (sibling, over_x, over_y):
            pl.semaphore_signal(barrier, inc=1, device_id={"lon": target}, device_id_type=MESH)

        @pl.when(has_above)
        def _():
            pl.semaphore_signal(barrier, inc=1, device_id={"lat": band + 1}, device_id_type=MESH)

        @pl.when(has_below)
        def _():
            pl.semaphore_signal(barrier, inc=1, device_id={"lat": band - 1}, device_id_type=MESH)

        def remote_copy(at, source, target, device):
            return pltpu.make_async_remote_copy(
                src_ref=source, dst_ref=target, send_sem=send.at[at], recv_sem=recv.at[at],
                device_id=device, device_id_type=MESH,
            )

        own = blocks.at[core]
        centre, frame = pl.ds(0, rows), pl.ds(rows, 2 * rim)
        to_above = remote_copy(0, own.at[pl.ds(rows - rim, rim)], own.at[pl.ds(rows + rim, rim)], {"lat": band + 1})
        to_below = remote_copy(1, own.at[pl.ds(0, rim)], own.at[pl.ds(rows, rim)], {"lat": band - 1})

        def three(first, part):
            return (
                remote_copy(first, own.at[part], own.at[part], {"lon": sibling}),
                remote_copy(first + 1, own.at[part], blocks.at[2 + core].at[part], {"lon": over_x}),
                remote_copy(first + 2, own.at[part], blocks.at[4 + core].at[part], {"lon": over_y}),
            )

        early, late = three(2, centre), three(5, frame)
        from_sibling = [
            remote_copy(at, blocks.at[other].at[part], blocks.at[other].at[part], {"lon": sibling})
            for at, part in ((2, centre), (5, frame))
        ]
        forward = [
            remote_copy(7 + k, blocks.at[2 * k + core], blocks.at[2 * k + core], {"lon": sibling}) for k in (1, 2, 3)
        ]
        arrive = [
            remote_copy(7 + k, blocks.at[2 * k + other], blocks.at[2 * k + other], {"lon": sibling}) for k in (1, 2, 3)
        ]
        across = remote_copy(
            11, blocks.at[4 - core], blocks.at[6 + core], {"lon": place + (over_x - place) * other + (over_y - place) * core}
        )

    flat = by_row(tokens_ref, rows, width)
    h_one = normalize(flat.astype(F32), gain_attn_ref[...]).astype(BF16)

    if remote:
        blocks[core, :rows] = h_one.reshape(rows, levels, cols, width)

        @pl.when(band == n_lat - 1)
        def _():
            blocks[core, rows : rows + rim] = jnp.zeros((rim, levels, cols, width), BF16)

        @pl.when(band == 0)
        def _():
            blocks[core, rows + rim :] = jnp.zeros((rim, levels, cols, width), BF16)

        pl.semaphore_wait(barrier, 3 + jnp.where(has_above, 1, 0) + jnp.where(has_below, 1, 0))
        pl.when(has_above)(to_above.start)
        pl.when(has_below)(to_below.start)
        for copy in early:
            copy.start()
        pl.when(has_above)(to_below.wait_recv)
        pl.when(has_below)(to_above.wait_recv)
        for copy in late:
            copy.start()

    fetch[0].wait()
    start_queries(h_one, esb_ref, w_qkv_ref, q_aug, heads, dim, rows)
    w_kt[...] = w_qkv_ref[:, width : 2 * width].T
    hot, row = start_state(k_aug, v_aug, top, acc, heads, dim, ext, rows)

    wide, offset = widths_ref[band], shifts_ref[band]
    key = lax.broadcasted_iota(jnp.int32, (1, span), 1)
    lat_row = band * rows - rim + (key // per_row + rim) % ext
    row_ok = (lat_row >= 0) & (lat_row < rows * n_lat)
    home = (place - offset) & (n_lon - 1)

    if remote:
        for copy in from_sibling:
            copy.wait_recv()

    def step(s, carry):
        if remote:

            @pl.when(s == 1)
            def _():
                early[1].wait_recv()
                late[1].wait_recv()
                forward[0].start()
                early[2].wait_recv()
                late[2].wait_recv()
                forward[1].start()
                across.start()
                arrive[0].wait_recv()

            @pl.when(s == 2)
            def _():
                arrive[1].wait_recv()
                across.wait_recv()
                forward[2].start()

            @pl.when(s == 3)
            def _():
                arrive[2].wait_recv()

            first = ((place // 2) ^ s) * 2
        else:
            first = 2 * s
        source = first + key // (ext * per_row)
        col_ok = (((source - offset) & (n_lon - 1)) ^ home) < wide
        mask = jnp.where(row_ok & col_ok, 0.0, NEG)
        block = blocks[pl.ds(pl.multiple_of(2 * s, 2), 2)].reshape(span, width)
        attend(
            block, mask, hot, row, w_kt, w_qkv_ref, q_aug, k_aug, v_aug,
            (scores_a, scores_b), (probs_a, probs_b), top, acc, heads, dim,
        )
        return carry

    lax.fori_loop(0, n_lon // 2, step, 0)
    for copy in fetch[1:]:
        copy.wait()
    flat = by_row(tokens_ref, rows, width)
    result = finish(flat, acc, w_out_ref, gain_mlp_ref, w_up_ref, w_down_ref, heads, dim)
    for r in range(rows):
        out_ref[:, r] = result[r * per_row : (r + 1) * per_row].reshape(levels, cols, width)
    if remote:
        pl.when(has_above)(to_above.wait_send)
        pl.when(has_below)(to_below.wait_send)
        for copy in (*early, *late, *forward, across):
            copy.wait_send()


def work_buffers(heads, count, width, span):
    return [
        pltpu.VMEM((heads, count, LANES), BF16),
        pltpu.VMEM((heads, LANES, span), BF16),
        pltpu.VMEM((width // LANES, span, 2 * LANES), BF16),
        pltpu.VMEM((count, span), F32),
        pltpu.VMEM((count, span), F32),
        pltpu.VMEM((count, span), BF16),
        pltpu.VMEM((count, span), BF16),
        pltpu.VMEM((heads, count, LANES), F32),
        pltpu.VMEM((heads, count, 2 * LANES), F32),
        pltpu.VMEM((width, width), BF16),
    ]


def bias_lanes(esb, dim):
    heads, ext = esb.shape
    lane = lax.broadcasted_iota(jnp.int32, (heads, LANES), 1) - 2 * dim
    used = (lane >= 0) & (lane < 3 * ext)
    bias = jnp.zeros((heads, LANES), F32)
    for e in range(ext):
        here = used & (lane % ext == e)
        bias = jnp.where(here, jnp.broadcast_to(esb[:, e : e + 1], (heads, LANES)), bias)
    bias = bias * math.log2(math.e)
    high = bias.astype(BF16).astype(F32)
    middle = (bias - high).astype(BF16).astype(F32)
    low = bias - high - middle
    pieces = jnp.where(lane < ext, high, jnp.where(lane < 2 * ext, middle, low))
    return jnp.where(lane == 3 * ext, 1.0, pieces)


def shards(tokens, gain_attn, w_qkv, esb, w_out, gain_mlp, w_up, w_down, widths, shifts):
    levels, rows, cols, width = tokens.shape
    heads, ext = esb.shape[1:]
    rim = (ext - rows) // 2
    dim = width // heads
    n_lon = lax.axis_size("lon")
    n_lat = lax.axis_size("lat")
    per_row = levels * cols
    span = 2 * ext * per_row
    remote = n_lon == 8
    operands = [tokens, esb, gain_attn, gain_mlp, widths, shifts, w_qkv, w_out, w_up, w_down]
    vmem = pl.BlockSpec(memory_space=pltpu.VMEM)
    smem = pl.BlockSpec(memory_space=pltpu.SMEM)
    specs = [vmem] * 4 + [smem] * 2 + [pl.BlockSpec(memory_space=pl.ANY)] * 4
    scratch = work_buffers(heads, rows * per_row, width, span)
    scratch += [pltpu.VMEM(w.shape, BF16) for w in operands[6:]] + [pltpu.SemaphoreType.DMA((4,))]
    params = dict(vmem_limit_bytes=58 * 1024 * 1024)
    if remote:
        scratch = [
            pltpu.VMEM((n_lon, ext, levels, cols, width), BF16),
            pltpu.SemaphoreType.DMA((12,)),
            pltpu.SemaphoreType.DMA((12,)),
        ] + scratch
        params.update(collective_id=0, has_side_effects=True)
    else:
        h_one = normalize(tokens.astype(F32), gain_attn).astype(BF16).transpose(1, 0, 2, 3)
        up = [(i, i + 1) for i in range(n_lat - 1)]
        down = [(i + 1, i) for i in range(n_lat - 1)]
        framed = jnp.concatenate(
            [h_one, lax.ppermute(h_one[:rim], "lat", down), lax.ppermute(h_one[rows - rim :], "lat", up)], axis=0
        )
        operands.append(lax.all_gather(framed, "lon", axis=0, tiled=False))
        specs.append(vmem)
    return pl.pallas_call(
        functools.partial(layer_kernel, heads, dim, ext, n_lon, n_lat, remote),
        out_shape=jax.ShapeDtypeStruct(tokens.shape, BF16),
        in_specs=specs,
        out_specs=vmem,
        scratch_shapes=scratch,
        compiler_params=pltpu.CompilerParams(**params),
    )(*operands)


def solution(mesh):
    placed = (P(None, "lat", "lon", None), P(), P(), P("lat", None, None), P(), P(), P(), P(), P(), P())
    return jax.shard_map(
        shards, mesh=mesh, in_specs=placed, out_specs=P(None, "lat", "lon", None), check_vma=False
    )
```

time: 402 us -> 54.4 us (0.14)
  local copies, waits for them, and re-layouts: 178 us -> 3.11 us
  matrix products: 110 us -> 0 us
  waiting for transfers between devices: 51.8 us -> 0 us
  Pallas kernels: 0 us -> 51.1 us
  other arithmetic: 37.1 us -> 0 us
  between operations: 16.6 us -> 0.01 us
  starting transfers between devices: 6.1 us -> 0 us
    add x4 -> x0, local copies, waits for them, and re-layouts: 121 us -> none  [attend_block(): scores.reshape(heads, count, levels, ext, ncols)]
    dot_general x6 -> x0, matrix products: 110 us -> none  [the longest x1 65.5 us: attend_block(): jnp.einsum('qhd,khd->hqk', queries, keys, preferred_element_type=jnp.floa...]
    pallas_call x0 -> x1, Pallas kernels: none -> 51.1 us  [shards(): pl.pallas_call(functools.partial(layer_kernel, heads, dim, ext, n_lon, n_...]
    all_gather x1 -> x0, waiting for transfers between devices: 48.3 us -> none  [shards(): block = lax.all_gather(framed, 'lon', axis=2, tiled=True)]
    reduce_sum x4 -> x0, other arithmetic: 32.6 us -> none  [the longest x1 30 us: attend_block(): total = jnp.sum(weights, axis=2)]
    another operation x2 -> x0, local copies, waits for them, and re-layouts: 23.3 us -> none
    reshape x2 -> x0, local copies, waits for them, and re-layouts: 19.3 us -> none  [the longest x1 9.64 us: attend_block(): keys = block[..., :width].reshape(-1, heads, dim)]
    slice x2 -> x0, local copies, waits for them, and re-layouts: 11.4 us -> none  [the longest x1 11.4 us: attend_block(): values = block[..., width:].reshape(-1, heads, dim)]
  transfers between devices with their start and end apart: 3 -> 0, of which waited for: 3 -> 0; matrix products, arithmetic and copies ran while one was open for 1% -> 0% of each run, Pallas kernels for 0% -> 0%
where the time goes in v1:
time: 54.4 us; the launch traced here: 54.2 us
  Pallas kernels  51.1 us (94%)
  local copies, waits for them, and re-layouts  3.11 us (6%)
    pallas_call x1, Pallas kernels, shards(): pl.pallas_call(functools.partial(layer_kernel, heads, dim, ext, n_lon, n_...  51.1 us
    unnamed x2, local copies, waits for them, and re-layouts  3.11 us

profile of v1, /device:TPU:1, one launch (start us, length us, event | category | flops | bytes accessed | tf_op | source)
XLA Modules:
  0.0 54.2 jit_solution(1471639551884892315)
XLA Ops:
  0.0 1.4 %copy.11.refs_1_ = f32[3,12,5]{2,1,0:T(8,128)} copy(f32[3,12,5]{1,0,2:T(4,128)} %param.13) | data formatting | bytes 1440 | tf_op args[3]
  1.4 51.1 %shard_map.100 = bf16[8,3,16,384]{3,2,1,0:T(8,128)(2,1)} custom-call(bf16[8,3,16,384]{3,2,1,0:T(8,128)(2,1)} %refs_0_.1, f32[3,12,5]{2,1,0:T(8,128)} %copy.11.refs_1_, f32[384]{0:T(512)} %refs_2_.1, f32[384]{0:T(512)} %refs_3_.1, s32[4]{0:T(128)} %refs_4_.1, s32[4]{0:T(128)} %refs_5_.1, bf16[384,1152]{1,0:T(8,128)(2,1)} %refs_6_.1, ...), custom_call_target="tpu_custom_call" | custom-call | tf_op jit(solution)/shard_map/pallas_call | solution.py:372
  52.5 1.7 %copy.13 = bf16[8,3,16,384]{3,2,1,0:T(8,128)(2,1)} copy(bf16[8,3,16,384]{3,2,1,0:T(8,128)(2,1)} %shard_map.100) | data formatting | bytes 589824

commit v2 on v1

--- a/solution.py
+++ b/solution.py
@@ -56,24 +56,21 @@
             q_aug[h, r * per_row : (r + 1) * per_row, :] = packed.astype(BF16)
 
 
-def start_state(k_aug, v_aug, top, acc, heads, dim, ext, rows):
+def start_state(k_aug, v_aug, top, acc, heads, dim):
     span = k_aug.shape[2]
-    per_row = LANES
-    row = lax.broadcasted_iota(jnp.int32, (16, span), 0)
-    key = lax.broadcasted_iota(jnp.int32, (16, span), 1)
-    place = (key // per_row + (ext - rows) // 2) % ext
-    hot = ((row % ext) == place) & (row < 3 * ext)
     k_aug[:, 2 * dim + 16 :, :] = jnp.zeros((heads, k_aug.shape[1] - 2 * dim - 16, span), BF16)
     v_aug[:, :, LANES:] = jnp.ones((v_aug.shape[0], span, LANES), BF16)
     top[...] = jnp.full(top.shape, LOW, F32)
     acc[...] = jnp.zeros(acc.shape, F32)
-    return hot.astype(F32), row
-
-
-def attend(block, mask, hot, row, w_kt, w_qkv_ref, q_aug, k_aug, v_aug, scores, probs, top, acc, heads, dim):
+
+
+def attend(block, mask, window_row, w_kt, w_qkv_ref, work, heads, dim, ext, between=None):
+    q_aug, k_aug, v_aug, scores, probs, alphas, top, acc = work
     span, width = block.shape
     count = q_aug.shape[1]
     group = LANES // dim
+    row = lax.broadcasted_iota(jnp.int32, (16, span), 0)
+    hot = jnp.where((row % ext == window_row) & (row < 3 * ext), 1.0, 0.0)
     extra = jnp.where(row == 15, jnp.broadcast_to(mask, row.shape), hot).astype(BF16)
     for g in range(width // LANES):
         keys = lax.dot_general(
@@ -82,32 +79,34 @@
         for j in range(group):
             h = g * group + j
             head = keys[j * dim : (j + 1) * dim, :]
-            k_aug[h, :dim, :] = head
-            k_aug[h, dim : 2 * dim, :] = head
-            k_aug[h, 2 * dim : 2 * dim + 16, :] = extra
-    values = dot(block, w_qkv_ref[:, 2 * width :]).astype(BF16)
+            k_aug[h, :dim, :span] = head
+            k_aug[h, dim : 2 * dim, :span] = head
+            k_aug[h, 2 * dim : 2 * dim + 16, :span] = extra
+    values = dot(block, w_qkv_ref[:, 2 * width :])
     for g in range(width // LANES):
-        v_aug[g, :, :LANES] = values[:, g * LANES : (g + 1) * LANES]
+        v_aug[g, :span, :LANES] = values[:, g * LANES : (g + 1) * LANES].astype(BF16)
 
     def product(h, slot):
-        scores[slot][...] = dot(q_aug[h], k_aug[h])
+        scores[slot][:, :span] = dot(q_aug[h], k_aug[h, :, :span])
 
     def soften(h, slot):
         step = 32
         for at in range(0, count, step):
-            s = scores[slot][at : at + step, :]
+            s = scores[slot][at : at + step, :span]
             old = top[h, at : at + step, :]
             new = jnp.maximum(old, jnp.max(s, axis=1, keepdims=True))
             top[h, at : at + step, :] = new
-            alpha = jnp.exp2(old - new)
+            alphas[slot][at : at + step, :] = jnp.exp2(old - new)
             wide = jnp.concatenate([new] * (span // LANES), axis=1)
-            probs[slot][at : at + step, :] = jnp.exp2(s - wide).astype(BF16)
-            acc[h, at : at + step, :] = acc[h, at : at + step, :] * jnp.concatenate([alpha, alpha], axis=1)
-        acc[h] += dot(probs[slot][...], v_aug[h // group])
+            probs[slot][at : at + step, :span] = jnp.exp2(s - wide).astype(BF16)
+        fade = jnp.concatenate([alphas[slot][...]] * 2, axis=1)
+        acc[h] = acc[h] * fade + dot(probs[slot][:, :span], v_aug[h // group, :span, :])
 
     product(0, 0)
 
     def pair(i, carry):
+        if between is not None:
+            between(i)
         product(2 * i + 1, 1)
         soften(2 * i, 0)
         product(jnp.minimum(2 * i + 2, heads - 1), 0)
@@ -149,12 +148,12 @@
     else:
         blocks, out_ref = refs[:2]
         refs = refs[2:]
-    q_aug, k_aug, v_aug, scores_a, scores_b, probs_a, probs_b, top, acc, w_kt = refs[:10]
-    w_qkv_ref, w_out_ref, w_up_ref, w_down_ref, loads = refs[10:]
+    q_aug, k_aug, v_aug, scores_a, scores_b, probs_a, probs_b, alpha_a, alpha_b, top, acc, w_kt = refs[:12]
+    w_qkv_ref, w_out_ref, w_up_ref, w_down_ref, loads = refs[12:]
     levels, rows, cols, width = tokens_ref.shape
     per_row = levels * cols
     rim = (ext - rows) // 2
-    span = k_aug.shape[2]
+    work = (q_aug, k_aug, v_aug, (scores_a, scores_b), (probs_a, probs_b), (alpha_a, alpha_b), top, acc)
     band = lax.axis_index("lat")
     place = lax.axis_index("lon")
     core = place % 2
@@ -205,14 +204,18 @@
             remote_copy(at, blocks.at[other].at[part], blocks.at[other].at[part], {"lon": sibling})
             for at, part in ((2, centre), (5, frame))
         ]
+        whole = pl.ds(0, ext)
+        passed = ((8, 1, centre), (9, 2, centre), (10, 1, frame), (11, 2, frame), (12, 3, whole))
         forward = [
-            remote_copy(7 + k, blocks.at[2 * k + core], blocks.at[2 * k + core], {"lon": sibling}) for k in (1, 2, 3)
+            remote_copy(at, blocks.at[2 * k + core].at[part], blocks.at[2 * k + core].at[part], {"lon": sibling})
+            for at, k, part in passed
         ]
         arrive = [
-            remote_copy(7 + k, blocks.at[2 * k + other], blocks.at[2 * k + other], {"lon": sibling}) for k in (1, 2, 3)
+            remote_copy(at, blocks.at[2 * k + other].at[part], blocks.at[2 * k + other].at[part], {"lon": sibling})
+            for at, k, part in passed
         ]
         across = remote_copy(
-            11, blocks.at[4 - core], blocks.at[6 + core], {"lon": place + (over_x - place) * other + (over_y - place) * core}
+            13, blocks.at[4 - core], blocks.at[6 + core], {"lon": place + (over_x - place) * other + (over_y - place) * core}
         )
 
     flat = by_row(tokens_ref, rows, width)
@@ -234,64 +237,102 @@
         pl.when(has_below)(to_below.start)
         for copy in early:
             copy.start()
-        pl.when(has_above)(to_below.wait_recv)
-        pl.when(has_below)(to_above.wait_recv)
-        for copy in late:
-            copy.start()
 
     fetch[0].wait()
     start_queries(h_one, esb_ref, w_qkv_ref, q_aug, heads, dim, rows)
     w_kt[...] = w_qkv_ref[:, width : 2 * width].T
-    hot, row = start_state(k_aug, v_aug, top, acc, heads, dim, ext, rows)
+    start_state(k_aug, v_aug, top, acc, heads, dim)
 
     wide, offset = widths_ref[band], shifts_ref[band]
-    key = lax.broadcasted_iota(jnp.int32, (1, span), 1)
-    lat_row = band * rows - rim + (key // per_row + rim) % ext
-    row_ok = (lat_row >= 0) & (lat_row < rows * n_lat)
     home = (place - offset) & (n_lon - 1)
 
-    if remote:
-        for copy in from_sibling:
-            copy.wait_recv()
-
-    def step(s, carry):
+    def describe(pieces):
+        masks, lines, parts = [], [], []
+        for pair, at, lines_in in pieces:
+            here = lines_in * per_row
+            key = lax.broadcasted_iota(jnp.int32, (1, 2 * here), 1)
+            line = (at + (key % here) // per_row + rim) % ext
+            first = ((place // 2) ^ pair) * 2 if remote else 2 * pair
+            source = first + key // here
+            lat_row = band * rows - rim + line
+            row_ok = (lat_row >= 0) & (lat_row < rows * n_lat)
+            col_ok = (((source - offset) & (n_lon - 1)) ^ home) < wide
+            masks.append(jnp.where(row_ok & col_ok, 0.0, NEG))
+            lines.append(line)
+            tokens = blocks[pl.ds(pl.multiple_of(2 * pair, 2), 2), at : at + lines_in]
+            parts.append(tokens.reshape(2 * here, width))
+        join = lambda x, axis: jnp.concatenate(x, axis=axis) if len(x) > 1 else x[0]
+        return join(parts, 0), join(masks, 1), join(lines, 1)
+
+    def centres(s, between=None):
+        attend(*describe([(s, 0, rows)]), w_kt, w_qkv_ref, work, heads, dim, ext, between)
+
+    def rest(s, between=None):
+        a = 2 * (s - n_pairs // 2)
+        pieces = [(a, rows, 2 * rim), (a + 1, rows, 2 * rim), (s, 0, rows)]
+        attend(*describe(pieces), w_kt, w_qkv_ref, work, heads, dim, ext, between)
+
+    n_pairs = n_lon // 2
+    if remote:
+        from_sibling[0].wait_recv()
+
+    def first_half(s, carry):
+        def between(i):
+            rim_time = (s == 0) & (i == 1)
+            pl.when(rim_time & has_above)(to_below.wait_recv)
+            pl.when(rim_time & has_below)(to_above.wait_recv)
+
+            @pl.when(rim_time)
+            def _():
+                for copy in late:
+                    copy.start()
+
+            @pl.when((s == 1) & (i == 3))
+            def _():
+                early[2].wait_recv()
+                forward[1].start()
+                late[1].wait_recv()
+                forward[2].start()
+                late[2].wait_recv()
+                forward[3].start()
+                across.start()
+
         if remote:
 
             @pl.when(s == 1)
             def _():
                 early[1].wait_recv()
-                late[1].wait_recv()
                 forward[0].start()
-                early[2].wait_recv()
-                late[2].wait_recv()
-                forward[1].start()
-                across.start()
                 arrive[0].wait_recv()
 
+        centres(s, between if remote else None)
+        return carry
+
+    def second_half(s, carry):
+        def between(i):
+            @pl.when((s == 2) & (i == 4))
+            def _():
+                across.wait_recv()
+                forward[4].start()
+
+        if remote:
+
             @pl.when(s == 2)
             def _():
+                from_sibling[1].wait_recv()
                 arrive[1].wait_recv()
-                across.wait_recv()
-                forward[2].start()
+                arrive[2].wait_recv()
+                arrive[3].wait_recv()
 
             @pl.when(s == 3)
             def _():
-                arrive[2].wait_recv()
-
-            first = ((place // 2) ^ s) * 2
-        else:
-            first = 2 * s
-        source = first + key // (ext * per_row)
-        col_ok = (((source - offset) & (n_lon - 1)) ^ home) < wide
-        mask = jnp.where(row_ok & col_ok, 0.0, NEG)
-        block = blocks[pl.ds(pl.multiple_of(2 * s, 2), 2)].reshape(span, width)
-        attend(
-            block, mask, hot, row, w_kt, w_qkv_ref, q_aug, k_aug, v_aug,
-            (scores_a, scores_b), (probs_a, probs_b), top, acc, heads, dim,
-        )
+                arrive[4].wait_recv()
+
+        rest(s, between if remote else None)
         return carry
 
-    lax.fori_loop(0, n_lon // 2, step, 0)
+    lax.fori_loop(0, n_pairs // 2, first_half, 0)
+    lax.fori_loop(n_pairs // 2, n_pairs, second_half, 0)
     for copy in fetch[1:]:
         copy.wait()
     flat = by_row(tokens_ref, rows, width)
@@ -314,6 +355,8 @@
         pltpu.VMEM((count, span), F32),
         pltpu.VMEM((count, span), BF16),
         pltpu.VMEM((count, span), BF16),
+        pltpu.VMEM((count, LANES), F32),
+        pltpu.VMEM((count, LANES), F32),
         pltpu.VMEM((heads, count, LANES), F32),
         pltpu.VMEM((heads, count, 2 * LANES), F32),
         pltpu.VMEM((width, width), BF16),
@@ -344,7 +387,7 @@
     n_lon = lax.axis_size("lon")
     n_lat = lax.axis_size("lat")
     per_row = levels * cols
-    span = 2 * ext * per_row
+    span = 2 * (rows + 4 * rim) * per_row
     remote = n_lon == 8
     operands = [tokens, esb, gain_attn, gain_mlp, widths, shifts, w_qkv, w_out, w_up, w_down]
     vmem = pl.BlockSpec(memory_space=pltpu.VMEM)
@@ -356,8 +399,8 @@
     if remote:
         scratch = [
             pltpu.VMEM((n_lon, ext, levels, cols, width), BF16),
-            pltpu.SemaphoreType.DMA((12,)),
-            pltpu.SemaphoreType.DMA((12,)),
+            pltpu.SemaphoreType.DMA((14,)),
+            pltpu.SemaphoreType.DMA((14,)),
         ] + scratch
         params.update(collective_id=0, has_side_effects=True)
     else:

time: 54.4 us -> 53 us (0.974)
  Pallas kernels: 51.1 us -> 49.6 us
    pallas_call x1, Pallas kernels: 51.1 us -> 49.6 us  [shards(): pl.pallas_call(functools.partial(layer_kernel, heads, dim, ext, n_lon, n_...]
where the time goes in v2:
time: 53 us; the launch traced here: 52.8 us
  Pallas kernels  49.6 us (94%)
  local copies, waits for them, and re-layouts  3.11 us (6%)
    pallas_call x1, Pallas kernels, shards(): pl.pallas_call(functools.partial(layer_kernel, heads, dim, ext, n_lon, n_...  49.6 us
    unnamed x2, local copies, waits for them, and re-layouts  3.11 us

profile of v2, /device:TPU:1, one launch (start us, length us, event | category | flops | bytes accessed | tf_op | source)
XLA Modules:
  0.0 52.8 jit_solution(4581379043388055286)
XLA Ops:
  0.0 1.4 %copy.11.refs_1_ = f32[3,12,5]{2,1,0:T(8,128)} copy(f32[3,12,5]{1,0,2:T(4,128)} %param.13) | data formatting | bytes 1440 | tf_op args[3]
  1.4 49.6 %shard_map.100 = bf16[8,3,16,384]{3,2,1,0:T(8,128)(2,1)} custom-call(bf16[8,3,16,384]{3,2,1,0:T(8,128)(2,1)} %refs_0_.1, f32[3,12,5]{2,1,0:T(8,128)} %copy.11.refs_1_, f32[384]{0:T(512)} %refs_2_.1, f32[384]{0:T(512)} %refs_3_.1, s32[4]{0:T(128)} %refs_4_.1, s32[4]{0:T(128)} %refs_5_.1, bf16[384,1152]{1,0:T(8,128)(2,1)} %refs_6_.1, ...), custom_call_target="tpu_custom_call" | custom-call | tf_op jit(solution)/shard_map/pallas_call | solution.py:415
  51.1 1.7 %copy.13 = bf16[8,3,16,384]{3,2,1,0:T(8,128)(2,1)} copy(bf16[8,3,16,384]{3,2,1,0:T(8,128)(2,1)} %shard_map.100) | data formatting | bytes 589824
